TPU v7x, 32 devices: a whole 2x2x4 slice. The times are simulated.
32 devices in a mesh: section: 1, expert: 32 (over z, y, x, core).
Axes of the slice: x: 2, y: 2, z: 4, core: 2. Of those that a mesh axis runs over, the one named last changes fastest.
Arguments:
- feat_saved: bfloat16 [1, 2, 4096, 1024], P('section', None, 'expert'), may hold values from -6 to 6
- out_grad: bfloat16 [2, 4096, 1024], P(None, 'expert'), may hold values from -6 to 6
- lengths: int32 [2, 32], P(None, 'expert'), may hold values from 32 to 128, as said below
- expert_ids: int32 [1, 2, 4096], P('section', None, 'expert'), may hold values from 0 to 31, as said below
- slot_ids: int32 [1, 2, 4096], P('section', None, 'expert'), may hold values from 0 to 5, as said below
- expert_preact: bfloat16 [1, 2, 6144, 640], P('section', None, 'expert'), may hold values from -6 to 6
- conv_weight: bfloat16 [1, 32, 1024], P('section'), may hold values from -0.5 to 0.5
- norm_gain: bfloat16 [1, 1024], P('section'), may hold values from 0.5 to 1.5
- centroids: bfloat16 [1, 32, 1024], P('section'), may hold values from -0.375 to 0.375
- w_in: bfloat16 [1, 32, 1024, 640], P('section', 'expert'), may hold values from -0.1875 to 0.1875
- w_out: bfloat16 [1, 32, 640, 1024], P('section', 'expert'), may hold values from -0.25 to 0.25
Outputs:
- section_grads: bfloat16 [1, 2, 4096, 1024], P('section', None, 'expert')
Inputs may be any that keep to these rules, and one draw needn't show every extreme that they name: `expert_ids`: in every block and micro-batch, the 128 frames of one utterance name each expert at most 6 times, and one expert is named exactly 6 times by the frames of every utterance. `slot_ids`: within one utterance's frames of one block and micro-batch, the frames that name the same expert hold the slots 0, 1, ... up to their count less one, each once. `lengths`: in every micro-batch at least one utterance has all 128 frames.
All inputs are finite; a program needn't handle non-finite values.
Results may differ from a plain program's by a relative error of at most 0.02.
Values may be sent and summed in bfloat16 or wider, within the bound.
A program may use at most 64 MiB of HBM per device.

v0:
```python
import functools
import math

import jax
import jax.numpy as jnp
from jax import lax
from jax.experimental import pallas as pl
from jax.experimental.pallas import tpu as pltpu
from jax.sharding import PartitionSpec as P

LANES = 128
SUB = 8
MESH = pl.DeviceIdType.MESH


def contract_last(left, right):
    return lax.dot_general(
        left, right, (((1,), (1,)), ((), ())), preferred_element_type=jnp.float32
    )


def to_column(row):
    size = row.shape[1]
    same = lax.broadcasted_iota(jnp.int32, (size, size), 0) == lax.broadcasted_iota(
        jnp.int32, (size, size), 1
    )
    wide = jnp.broadcast_to(row.astype(jnp.float32), (size, size))
    return jnp.sum(jnp.where(same, wide, 0.0), axis=1, keepdims=True).astype(jnp.int32)


def kernel(
    axis,
    n,
    slot_cap,
    length_hbm,
    routed_hbm,
    slot_hbm,
    conv_hbm,
    gain_hbm,
    cent_hbm,
    feat_hbm,
    grad_hbm,
    preact_hbm,
    w_in_hbm,
    w_out_hbm,
    out_ref,
    length_ref,
    routed_ref,
    slot_ref,
    conv_ref,
    gain_ref,
    cent_ref,
    feat_ref,
    grad_ref,
    preact_ref,
    w_in_ref,
    w_out_ref,
    taps_ref,
    gain_f,
    send_ref,
    recv_ref,
    back_ref,
    home_ref,
    gate_send,
    gate_recv,
    turn_ref,
    rows_ref,
    pad_ref,
    resid_ref,
    slope_ref,
    cent_rows,
    gelu_ref,
    gelu_slope_ref,
    slot_back,
    load_sem,
    send_sem,
    recv_sem,
    back_sem,
    home_sem,
    gate_send_sem,
    gate_recv_sem,
):
    micro, frames, width = feat_ref.shape
    stride = next(k for k in range(n // 3 + 1, 2 * n) if math.gcd(k, n) == 1)
    chunks = width // LANES
    slots = n * slot_cap
    tap_count = conv_ref.shape[0]
    low = tap_count // 2
    experts = n
    gate_span = LANES // micro
    me = lax.axis_index(axis)

    barrier = pltpu.get_barrier_semaphore()

    def greet(step, carry):
        pl.semaphore_signal(
            barrier, inc=1, device_id={axis: lax.rem(me + step, n)}, device_id_type=MESH
        )
        return carry

    def load(src, dst, at):
        return pltpu.make_async_copy(src, dst, load_sem.at[at])

    routed_load = load(routed_hbm, routed_ref, 2 * micro + 3)
    slot_load = load(slot_hbm, slot_ref, 2 * micro + 4)
    small_loads = [
        load(conv_hbm, conv_ref, 2 * micro + 5),
        load(gain_hbm, gain_ref, 2 * micro + 6),
        load(cent_hbm, cent_ref, 2 * micro + 7),
        load(length_hbm, length_ref, 2 * micro + 8),
    ]
    grad_loads = [load(grad_hbm.at[m], grad_ref.at[m], m) for m in range(micro)]
    feat_loads = [load(feat_hbm.at[m], feat_ref.at[m], micro + m) for m in range(micro)]
    pre_load = load(preact_hbm, preact_ref, 2 * micro)
    out_load = load(w_out_hbm, w_out_ref, 2 * micro + 1)
    in_load = load(w_in_hbm, w_in_ref, 2 * micro + 2)
    for copy in (routed_load, slot_load, *grad_loads):
        copy.start()
    lax.fori_loop(1, n, greet, 0)
    for copy in (*small_loads, *feat_loads, pre_load, out_load, in_load):
        copy.start()

    def cols(c):
        return pl.ds(c * LANES, LANES)

    def to_blocks(rows, dst):
        for c in range(chunks):
            turn_ref[pl.ds(c, slots, stride=chunks), :] = rows[:, c * LANES : (c + 1) * LANES]
        dst[...] = turn_ref[...].astype(jnp.bfloat16).reshape(dst.shape)

    def from_blocks(src):
        turn_ref[...] = src[...].reshape(turn_ref.shape).astype(jnp.float32)
        for c in range(chunks):
            rows_ref[:, cols(c)] = turn_ref[pl.ds(c, slots, stride=chunks), :].astype(jnp.bfloat16)

    def exchange(src, dst, sent, got):
        def post(step, carry):
            peer = lax.rem(me + step * stride, n)
            pltpu.make_async_remote_copy(
                src_ref=src.at[peer],
                dst_ref=dst.at[me],
                send_sem=sent,
                recv_sem=got,
                device_id={axis: peer},
                device_id_type=MESH,
            ).start()
            return carry

        lax.fori_loop(1, n, post, 0)
        pltpu.make_async_copy(src.at[me], dst.at[me], got).start()

    def arrived(dst, got):
        pltpu.make_async_copy(dst, dst, got).wait()

    def departed(src, sent):
        part = src.at[pl.ds(0, n - 1)]
        pltpu.make_async_copy(part, part, sent).wait()

    def dispatch(m):
        exchange(send_ref.at[m], recv_ref.at[m], send_sem.at[m], recv_sem.at[m])

    routed_load.wait()
    slot_load.wait()
    for m in range(micro):
        grad_loads[m].wait()
        target = routed_ref[m : m + 1, :] * slot_cap + slot_ref[m : m + 1, :]
        onehot = (lax.broadcasted_iota(jnp.int32, (slots, frames), 0) == target).astype(
            jnp.float32
        ).astype(jnp.bfloat16)
        bucket = jnp.dot(onehot, grad_ref[m], preferred_element_type=jnp.float32)
        to_blocks(bucket, send_ref.at[m])
        if m == 0:
            pl.semaphore_wait(barrier, n - 1)
            dispatch(m)

    for copy in small_loads:
        copy.wait()

    for c in range(chunks):
        taps_ref[c] = conv_ref[:, cols(c)].astype(jnp.float32)
        gain_f[c] = gain_ref[:, cols(c)].astype(jnp.float32)
        pad_ref[c, 0:low, :] = jnp.zeros((low, LANES), jnp.float32)
        pad_ref[c, low + frames :, :] = jnp.zeros((tap_count - low, LANES), jnp.float32)

    def conv(c, start, tap_of):
        acc = jnp.zeros((frames, LANES), jnp.float32)
        reach = (tap_count - 1) // SUB * SUB
        for offset in range(start, start + SUB):
            rows = pad_ref[c, offset : offset + frames + reach, :]
            for first in range(0, reach + 1, SUB):
                k = tap_of(offset + first)
                acc = acc + taps_ref[c, k : k + 1, :] * rows[first : first + frames, :]
        return acc

    frame_at = lax.broadcasted_iota(jnp.int32, (frames, 1), 0)

    masks, inv_all, gate_all, exp_all, slot_all, slot_hot = [], [], [], [], [], []
    for m in range(micro):
        feat_loads[m].wait()
        mask = (frame_at < length_ref[0, m]).astype(jnp.float32)
        routed = to_column(routed_ref[m : m + 1, :])
        slot_pos = to_column(slot_ref[m : m + 1, :])
        exp_hot = (
            lax.broadcasted_iota(jnp.int32, (frames, experts), 1) == routed
        ).astype(jnp.float32)
        cent_rows[m] = jnp.dot(
            exp_hot.astype(jnp.bfloat16), cent_ref[...], preferred_element_type=jnp.float32
        ).astype(jnp.bfloat16)

        def ahead(c, square):
            lanes = pl.ds(pl.multiple_of(c * LANES, LANES), LANES)
            feats = feat_ref[m, :, lanes].astype(jnp.float32)
            pad_ref[c, low : low + frames, :] = feats * mask
            acc = conv(c, 0, lambda first: first)
            sig = jax.nn.sigmoid(acc)
            resid = feats + mask * acc * sig
            resid_ref[m, c] = resid
            slope_ref[m, c] = mask * sig * (1.0 + acc * (1.0 - sig))
            return square + resid * resid

        square = lax.fori_loop(0, chunks, ahead, jnp.zeros((frames, LANES), jnp.float32))
        if m + 1 < micro:
            dispatch(m + 1)
        inv_rms = lax.rsqrt(jnp.sum(square, axis=1, keepdims=True) * (1.0 / width) + 1e-06)

        def scoring(c, total):
            lanes = pl.ds(pl.multiple_of(c * LANES, LANES), LANES)
            normed = (resid_ref[m, c] * inv_rms * gain_f[c]).astype(jnp.bfloat16)
            return total + normed.astype(jnp.float32) * cent_rows[m, :, lanes].astype(jnp.float32)

        score = lax.fori_loop(0, chunks, scoring, jnp.zeros((frames, LANES), jnp.float32))
        gate_all.append(jax.nn.sigmoid(jnp.sum(score, axis=1, keepdims=True)))
        masks.append(mask)
        inv_all.append(inv_rms)
        exp_all.append(exp_hot)
        slot_all.append(slot_pos)
        slot_hot.append(
            (
                lax.broadcasted_iota(jnp.int32, (frames, slots), 1)
                == routed * slot_cap + slot_pos
            ).astype(jnp.float32).astype(jnp.bfloat16)
        )

        if m == 0:
            pre_load.wait()
        act = preact_ref[m].astype(jnp.float32)
        cdf = 0.5 * (1.0 + lax.erf(act * (1.0 / math.sqrt(2.0))))
        gelu_ref[m] = act * cdf
        gelu_slope_ref[m] = cdf + act * jnp.exp(-0.5 * act * act) * (
            1.0 / math.sqrt(2.0 * math.pi)
        )

    out_load.wait()
    in_load.wait()
    gate_rows = jnp.zeros((n, LANES), jnp.float32)
    slot_id = lax.broadcasted_iota(jnp.int32, (slots, LANES), 0)
    lane_id = lax.broadcasted_iota(jnp.int32, (slots, LANES), 1)
    group_first = lax.broadcasted_iota(jnp.int32, (n, slots), 0) * slot_cap
    group_slot = lax.broadcasted_iota(jnp.int32, (n, slots), 1)
    grouped = jnp.logical_and(
        group_slot >= group_first, group_slot < group_first + slot_cap
    ).astype(jnp.float32)
    for m in range(micro):
        arrived(recv_ref.at[m], recv_sem.at[m])
        from_blocks(recv_ref.at[m])
        hidden = contract_last(rows_ref[...], w_out_ref[...])
        gate = jnp.sum(hidden * gelu_ref[m], axis=1, keepdims=True)
        pre_grad = (hidden * gelu_slope_ref[m]).astype(jnp.bfloat16)
        spread = jnp.where(lax.rem(slot_id, slot_cap) + m * gate_span == lane_id, gate, 0.0)
        gate_rows = gate_rows + jnp.dot(
            grouped, spread, preferred_element_type=jnp.float32, precision=lax.Precision.HIGHEST
        )
        if m == micro - 1:
            gate_send[...] = gate_rows.reshape(gate_send.shape)
            exchange(gate_send, gate_recv, gate_send_sem, gate_recv_sem)
        to_blocks(contract_last(pre_grad, w_in_ref[...]), back_ref.at[m])
        exchange(back_ref.at[m], home_ref.at[m], back_sem.at[m], home_sem.at[m])

    arrived(gate_recv, gate_recv_sem)
    frame_lane = lax.broadcasted_iota(jnp.int32, (frames, LANES), 1)
    for m in range(micro):
        mask, inv_rms, gate_val = masks[m], inv_all[m], gate_all[m]
        picked = jnp.dot(
            exp_all[m],
            gate_recv[...].reshape(n, LANES),
            preferred_element_type=jnp.float32,
            precision=lax.Precision.HIGHEST,
        )
        gate_grad = jnp.sum(
            jnp.where(frame_lane == slot_all[m] + m * gate_span, picked, 0.0),
            axis=1,
            keepdims=True,
        )
        cent_scale = gate_val * (1.0 - gate_val) * gate_grad
        arrived(home_ref.at[m], home_sem.at[m])
        from_blocks(home_ref.at[m])
        slot_back[...] = jnp.dot(slot_hot[m], rows_ref[...], preferred_element_type=jnp.float32)

        def scaling(c, total):
            lanes = pl.ds(pl.multiple_of(c * LANES, LANES), LANES)
            grad = gate_val * slot_back[:, lanes] + cent_scale * cent_rows[m, :, lanes].astype(
                jnp.float32
            )
            scaled = grad * gain_f[c]
            slot_back[:, lanes] = scaled
            return total + resid_ref[m, c] * scaled

        total = lax.fori_loop(0, chunks, scaling, jnp.zeros((frames, LANES), jnp.float32))
        mean = jnp.sum(total, axis=1, keepdims=True) * (1.0 / width)
        back_scale = inv_rms * inv_rms * inv_rms * mean

        def finish(c, carry):
            lanes = pl.ds(pl.multiple_of(c * LANES, LANES), LANES)
            resid_grad = (
                grad_ref[m, :, lanes].astype(jnp.float32)
                + inv_rms * slot_back[:, lanes]
                - resid_ref[m, c] * back_scale
            )
            pad_ref[c, low : low + frames, :] = slope_ref[m, c] * resid_grad
            acc = conv(c, 1, lambda first: 2 * low - first)
            out_ref[m, :, lanes] = (resid_grad + mask * acc).astype(jnp.bfloat16)
            return carry

        lax.fori_loop(0, chunks, finish, 0)

    for m in range(micro):
        departed(send_ref.at[m], send_sem.at[m])
        departed(back_ref.at[m], back_sem.at[m])
    departed(gate_send, gate_send_sem)


def block_grads(
    grads, feats, lengths, routed, slot_pos, preact, conv_k, gain, cent, weight_in, weight_out
):
    micro, frames, width = feats.shape
    n = lax.axis_size("expert")
    hidden = weight_in.shape[1]
    cap = preact.shape[1] // n
    whole_rows = 16 * LANES // math.gcd(16 * LANES, width)
    slot_cap = -(-cap // whole_rows) * whole_rows
    if slot_cap != cap:
        preact = jnp.pad(
            preact.reshape(micro, n, cap, hidden), ((0, 0), (0, 0), (0, slot_cap - cap), (0, 0))
        ).reshape(micro, n * slot_cap, hidden)
    slots = n * slot_cap
    chunks = width // LANES
    taps = conv_k.shape[0]
    block = (n, slot_cap * chunks, LANES)
    bf16, f32 = jnp.bfloat16, jnp.float32
    lengths = lengths.reshape(1, micro)
    held = (
        lengths, routed, slot_pos, conv_k, gain, cent, feats, grads, preact, weight_in, weight_out
    )
    operands = [pltpu.with_memory_space_constraint(x, pltpu.HBM) for x in held]
    in_hbm = pl.BlockSpec(memory_space=pltpu.HBM)
    dma = pltpu.SemaphoreType.DMA
    flops = micro * (4 * slots * width * hidden + 4 * frames * width * (taps + slots))
    return pl.pallas_call(
        functools.partial(kernel, "expert", n, slot_cap),
        out_shape=jax.ShapeDtypeStruct((micro, frames, width), bf16),
        in_specs=[in_hbm] * 11,
        out_specs=pl.BlockSpec(memory_space=pltpu.VMEM),
        scratch_shapes=[
            pltpu.SMEM((1, micro), jnp.int32),
            pltpu.VMEM((micro, frames), jnp.int32),
            pltpu.VMEM((micro, frames), jnp.int32),
            pltpu.VMEM((taps, width), bf16),
            pltpu.VMEM((1, width), bf16),
            pltpu.VMEM((n, width), bf16),
            pltpu.VMEM((micro, frames, width), bf16),
            pltpu.VMEM((micro, frames, width), bf16),
            pltpu.VMEM((micro, slots, hidden), bf16),
            pltpu.VMEM((width, hidden), bf16),
            pltpu.VMEM((hidden, width), bf16),
            pltpu.VMEM((chunks, taps, LANES), f32),
            pltpu.VMEM((chunks, 1, LANES), f32),
            pltpu.VMEM((micro, *block), bf16),
            pltpu.VMEM((micro, *block), bf16),
            pltpu.VMEM((micro, *block), bf16),
            pltpu.VMEM((micro, *block), bf16),
            pltpu.VMEM((n, 1, LANES), f32),
            pltpu.VMEM((n, 1, LANES), f32),
            pltpu.VMEM((slots * chunks, LANES), f32),
            pltpu.VMEM((slots, width), bf16),
            pltpu.VMEM((chunks, frames + taps, LANES), f32),
            pltpu.VMEM((micro, chunks, frames, LANES), f32),
            pltpu.VMEM((micro, chunks, frames, LANES), f32),
            pltpu.VMEM((micro, frames, width), bf16),
            pltpu.VMEM((micro, slots, hidden), f32),
            pltpu.VMEM((micro, slots, hidden), f32),
            pltpu.VMEM((frames, width), f32),
            dma((2 * micro + 9,)),
            dma((micro,)),
            dma((micro,)),
            dma((micro,)),
            dma((micro,)),
            dma,
            dma,
        ],
        compiler_params=pltpu.CompilerParams(
            collective_id=0, has_side_effects=True, vmem_limit_bytes=32 * 1024 * 1024
        ),
        cost_estimate=pl.CostEstimate(
            flops=flops, bytes_accessed=8 * 1024 * 1024, transcendentals=0
        ),
    )(*operands)


def on_device(
    feat_saved,
    out_grad,
    lengths,
    expert_ids,
    slot_ids,
    expert_preact,
    conv_weight,
    norm_gain,
    centroids,
    w_in,
    w_out,
):
    section_count = lax.axis_size("section")
    micro_count = out_grad.shape[0]
    feats, routed, slots, preact = feat_saved[0], expert_ids[0], slot_ids[0], expert_preact[0]
    fixed = (conv_weight[0], norm_gain, centroids[0], w_in[0, 0], w_out[0, 0])
    if section_count == 1:
        return block_grads(out_grad, feats, lengths, routed, slots, preact, *fixed)[None]

    section_idx = lax.axis_index("section")
    route = [(i + 1, i) for i in range(section_count - 1)]

    def one_tick(tick_idx, carry):
        incoming, grads = carry
        micro_pos = tick_idx - (section_count - 1 - section_idx)
        is_valid = jnp.logical_and(micro_pos >= 0, micro_pos < micro_count)
        micro_sel = jnp.clip(micro_pos, 0, micro_count - 1)

        def pick(array):
            return lax.dynamic_slice_in_dim(array, micro_sel, 1, 0)

        grad_in = jnp.where(section_idx == section_count - 1, pick(out_grad), incoming)
        new_grad = block_grads(
            grad_in, pick(feats), pick(lengths), pick(routed), pick(slots), pick(preact), *fixed
        )
        updated = lax.dynamic_update_slice_in_dim(grads, new_grad, micro_sel, 0)
        grads = jnp.where(is_valid, updated, grads)
        return (lax.ppermute(new_grad, "section", route), grads)

    start = (jnp.zeros((1, *out_grad.shape[1:]), jnp.bfloat16), jnp.zeros_like(out_grad))
    _, grads = lax.fori_loop(0, section_count + micro_count - 1, one_tick, start)
    return grads[None]


def solution(mesh):
    in_specs = (
        P("section", None, "expert", None),
        P(None, "expert", None),
        P(None, "expert"),
        P("section", None, "expert"),
        P("section", None, "expert"),
        P("section", None, "expert", None),
        P("section", None, None),
        P("section", None),
        P("section", None, None),
        P("section", "expert", None, None),
        P("section", "expert", None, None),
    )
    out_specs = P("section", None, "expert", None)
    return jax.shard_map(
        on_device, mesh=mesh, in_specs=in_specs, out_specs=out_specs, check_vma=False
    )
```

profile of v0, /device:TPU:0, one launch (start us, length us, event | category | flops | bytes accessed | tf_op | source)
XLA Modules:
  0.0 45.7 jit_solution(1188559031870989478)
XLA Ops:
  0.0 44.9 %shard_map.109 = bf16[2,128,1024]{2,1,0:T(8,128)(2,1)S(1)} custom-call(s32[1,2]{1,0:T(1,128)} %bitcast.19, s32[2,128]{1,0:T(2,128)} %bitcast.17, s32[2,128]{1,0:T(2,128)} %bitcast.18, bf16[32,1024]{1,0:T(8,128)(2,1)} %bitcast.15, bf16[1,1024]{1,0:T(2,128)(2,1)} %gain_hbm.1, bf16[32,1024]{1,0:T(8,128)(2,1)} %bitcast.16, bf16[2,128,1024]{2,1,0:T(8,128)(2,1)} %bitcast.13, ...), custom_call_target="tpu_custom_call" | custom-call | flops 1241513984 | bytes 8388608 | tf_op jit(solution)/shard_map/pallas_call | solution.py:358
  44.9 0.8 %copy.13 = bf16[1,2,128,1024]{3,2,1,0:T(8,128)(2,1)} copy(bf16[1,2,128,1024]{3,2,1,0:T(8,128)(2,1)S(1)} %bitcast.10) | data formatting | bytes 1048576
where the time goes:
time: 45.8 us; the launch traced here: 45.7 us
  Pallas kernels  44.9 us (98%)
  local copies, waits for them, and re-layouts  0.8 us (2%)
    pallas_call x1, Pallas kernels, block_grads(): pl.pallas_call(functools.partial(kernel, 'expert', n, slot_cap), out_shap...  44.9 us

commit v1 on v0

--- a/solution.py
+++ b/solution.py
@@ -195,7 +195,7 @@
     frame_at = lax.broadcasted_iota(jnp.int32, (frames, 1), 0)
 
     masks, inv_all, gate_all, exp_all, slot_all, slot_hot = [], [], [], [], [], []
-    for m in range(micro):
+    def forward(m):
         feat_loads[m].wait()
         mask = (frame_at < length_ref[0, m]).astype(jnp.float32)
         routed = to_column(routed_ref[m : m + 1, :])
@@ -250,9 +250,6 @@
             1.0 / math.sqrt(2.0 * math.pi)
         )
 
-    out_load.wait()
-    in_load.wait()
-    gate_rows = jnp.zeros((n, LANES), jnp.float32)
     slot_id = lax.broadcasted_iota(jnp.int32, (slots, LANES), 0)
     lane_id = lax.broadcasted_iota(jnp.int32, (slots, LANES), 1)
     group_first = lax.broadcasted_iota(jnp.int32, (n, slots), 0) * slot_cap
@@ -260,7 +257,10 @@
     grouped = jnp.logical_and(
         group_slot >= group_first, group_slot < group_first + slot_cap
     ).astype(jnp.float32)
-    for m in range(micro):
+    def expert(m, gate_rows):
+        if m == 0:
+            out_load.wait()
+            in_load.wait()
         arrived(recv_ref.at[m], recv_sem.at[m])
         from_blocks(recv_ref.at[m])
         hidden = contract_last(rows_ref[...], w_out_ref[...])
@@ -275,6 +275,12 @@
             exchange(gate_send, gate_recv, gate_send_sem, gate_recv_sem)
         to_blocks(contract_last(pre_grad, w_in_ref[...]), back_ref.at[m])
         exchange(back_ref.at[m], home_ref.at[m], back_sem.at[m], home_sem.at[m])
+        return gate_rows
+
+    gate_rows = jnp.zeros((n, LANES), jnp.float32)
+    for m in range(micro):
+        forward(m)
+        gate_rows = expert(m, gate_rows)
 
     arrived(gate_recv, gate_recv_sem)
     frame_lane = lax.broadcasted_iota(jnp.int32, (frames, LANES), 1)

time: 45.8 us -> 46 us (level)
  no operation moved by 1% of the time
where the time goes in v1:
time: 46 us; the launch traced here: 45.8 us
  Pallas kernels  45 us (98%)
  local copies, waits for them, and re-layouts  0.8 us (2%)
    pallas_call x1, Pallas kernels, block_grads(): pl.pallas_call(functools.partial(kernel, 'expert', n, slot_cap), out_shap...  45 us

profile of v1, /device:TPU:0, one launch (start us, length us, event | category | flops | bytes accessed | tf_op | source)
XLA Modules:
  0.0 45.8 jit_solution(16191137368852811531)
XLA Ops:
  0.0 45.0 %shard_map.109 = bf16[2,128,1024]{2,1,0:T(8,128)(2,1)S(1)} custom-call(s32[1,2]{1,0:T(1,128)} %bitcast.19, s32[2,128]{1,0:T(2,128)} %bitcast.17, s32[2,128]{1,0:T(2,128)} %bitcast.18, bf16[32,1024]{1,0:T(8,128)(2,1)} %bitcast.15, bf16[1,1024]{1,0:T(2,128)(2,1)} %gain_hbm.1, bf16[32,1024]{1,0:T(8,128)(2,1)} %bitcast.16, bf16[2,128,1024]{2,1,0:T(8,128)(2,1)} %bitcast.13, ...), custom_call_target="tpu_custom_call" | custom-call | flops 1241513984 | bytes 8388608 | tf_op jit(solution)/shard_map/pallas_call | solution.py:364
  45.1 0.8 %copy.13 = bf16[1,2,128,1024]{3,2,1,0:T(8,128)(2,1)} copy(bf16[1,2,128,1024]{3,2,1,0:T(8,128)(2,1)S(1)} %bitcast.10) | data formatting | bytes 1048576

commit v2 on v1

--- a/solution.py
+++ b/solution.py
@@ -133,7 +133,7 @@
         for c in range(chunks):
             rows_ref[:, cols(c)] = turn_ref[pl.ds(c, slots, stride=chunks), :].astype(jnp.bfloat16)
 
-    def exchange(src, dst, sent, got):
+    def exchange(src, dst, sent, got, beside=False):
         def post(step, carry):
             peer = lax.rem(me + step * stride, n)
             pltpu.make_async_remote_copy(
@@ -146,8 +146,11 @@
             ).start()
             return carry
 
+        pltpu.make_async_copy(src.at[me], dst.at[me], got).start()
+        if beside:
+            return post
         lax.fori_loop(1, n, post, 0)
-        pltpu.make_async_copy(src.at[me], dst.at[me], got).start()
+        return None
 
     def arrived(dst, got):
         pltpu.make_async_copy(dst, dst, got).wait()
@@ -156,8 +159,10 @@
         part = src.at[pl.ds(0, n - 1)]
         pltpu.make_async_copy(part, part, sent).wait()
 
-    def dispatch(m):
-        exchange(send_ref.at[m], recv_ref.at[m], send_sem.at[m], recv_sem.at[m])
+    def dispatch(m, beside=False):
+        return exchange(
+            send_ref.at[m], recv_ref.at[m], send_sem.at[m], recv_sem.at[m], beside
+        )
 
     routed_load.wait()
     slot_load.wait()
@@ -195,7 +200,7 @@
     frame_at = lax.broadcasted_iota(jnp.int32, (frames, 1), 0)
 
     masks, inv_all, gate_all, exp_all, slot_all, slot_hot = [], [], [], [], [], []
-    def forward(m):
+    def forward(m, posts):
         feat_loads[m].wait()
         mask = (frame_at < length_ref[0, m]).astype(jnp.float32)
         routed = to_column(routed_ref[m : m + 1, :])
@@ -207,7 +212,12 @@
             exp_hot.astype(jnp.bfloat16), cent_ref[...], preferred_element_type=jnp.float32
         ).astype(jnp.bfloat16)
 
+        share = (n - 1) // chunks
+
         def ahead(c, square):
+            for post in posts:
+                for j in range(share):
+                    post(1 + c * share + j, 0)
             lanes = pl.ds(pl.multiple_of(c * LANES, LANES), LANES)
             feats = feat_ref[m, :, lanes].astype(jnp.float32)
             pad_ref[c, low : low + frames, :] = feats * mask
@@ -219,8 +229,8 @@
             return square + resid * resid
 
         square = lax.fori_loop(0, chunks, ahead, jnp.zeros((frames, LANES), jnp.float32))
-        if m + 1 < micro:
-            dispatch(m + 1)
+        for post in posts:
+            lax.fori_loop(1 + chunks * share, n, post, 0)
         inv_rms = lax.rsqrt(jnp.sum(square, axis=1, keepdims=True) * (1.0 / width) + 1e-06)
 
         def scoring(c, total):
@@ -274,13 +284,18 @@
             gate_send[...] = gate_rows.reshape(gate_send.shape)
             exchange(gate_send, gate_recv, gate_send_sem, gate_recv_sem)
         to_blocks(contract_last(pre_grad, w_in_ref[...]), back_ref.at[m])
-        exchange(back_ref.at[m], home_ref.at[m], back_sem.at[m], home_sem.at[m])
-        return gate_rows
+        post = exchange(
+            back_ref.at[m], home_ref.at[m], back_sem.at[m], home_sem.at[m], m + 1 < micro
+        )
+        return gate_rows, post
 
     gate_rows = jnp.zeros((n, LANES), jnp.float32)
     for m in range(micro):
-        forward(m)
-        gate_rows = expert(m, gate_rows)
+        posts = [back_post] if m > 0 else []
+        if m + 1 < micro:
+            posts.append(dispatch(m + 1, True))
+        forward(m, posts)
+        gate_rows, back_post = expert(m, gate_rows)
 
     arrived(gate_recv, gate_recv_sem)
     frame_lane = lax.broadcasted_iota(jnp.int32, (frames, LANES), 1)

time: 46 us -> 45.8 us (level)
  no operation moved by 1% of the time
where the time goes in v2:
time: 45.8 us; the launch traced here: 45.7 us
  Pallas kernels  44.9 us (98%)
  local copies, waits for them, and re-layouts  0.8 us (2%)
    pallas_call x1, Pallas kernels, block_grads(): pl.pallas_call(functools.partial(kernel, 'expert', n, slot_cap), out_shap...  44.9 us

profile of v2, /device:TPU:0, one launch (start us, length us, event | category | flops | bytes accessed | tf_op | source)
XLA Modules:
  0.0 45.7 jit_solution(2609099693818375806)
XLA Ops:
  0.0 44.9 %shard_map.109 = bf16[2,128,1024]{2,1,0:T(8,128)(2,1)S(1)} custom-call(s32[1,2]{1,0:T(1,128)} %bitcast.19, s32[2,128]{1,0:T(2,128)} %bitcast.17, s32[2,128]{1,0:T(2,128)} %bitcast.18, bf16[32,1024]{1,0:T(8,128)(2,1)} %bitcast.15, bf16[1,1024]{1,0:T(2,128)(2,1)} %gain_hbm.1, bf16[32,1024]{1,0:T(8,128)(2,1)} %bitcast.16, bf16[2,128,1024]{2,1,0:T(8,128)(2,1)} %bitcast.13, ...), custom_call_target="tpu_custom_call" | custom-call | flops 1241513984 | bytes 8388608 | tf_op jit(solution)/shard_map/pallas_call | solution.py:379
  44.9 0.8 %copy.13 = bf16[1,2,128,1024]{3,2,1,0:T(8,128)(2,1)} copy(bf16[1,2,128,1024]{3,2,1,0:T(8,128)(2,1)S(1)} %bitcast.10) | data formatting | bytes 1048576

commit v3 on v0

--- a/solution.py
+++ b/solution.py
@@ -81,7 +81,6 @@
     gate_recv_sem,
 ):
     micro, frames, width = feat_ref.shape
-    stride = next(k for k in range(n // 3 + 1, 2 * n) if math.gcd(k, n) == 1)
     chunks = width // LANES
     slots = n * slot_cap
     tap_count = conv_ref.shape[0]
@@ -135,7 +134,8 @@
 
     def exchange(src, dst, sent, got):
         def post(step, carry):
-            peer = lax.rem(me + step * stride, n)
+            side = 2 * lax.rem(step + 1, 2) - 1
+            peer = lax.rem(me + n // 2 + side * lax.div(step, 2), n)
             pltpu.make_async_remote_copy(
                 src_ref=src.at[peer],
                 dst_ref=dst.at[me],

time: 45.8 us -> 46.7 us (1.020)
  Pallas kernels: 44.9 us -> 45.7 us
    pallas_call x1, Pallas kernels: 44.9 us -> 45.7 us  [block_grads(): pl.pallas_call(functools.partial(kernel, 'expert', n, slot_cap), out_shap...]
where the time goes in v3:
time: 46.7 us; the launch traced here: 46.5 us
  Pallas kernels  45.7 us (98%)
  local copies, waits for them, and re-layouts  0.8 us (2%)
    pallas_call x1, Pallas kernels, block_grads(): pl.pallas_call(functools.partial(kernel, 'expert', n, slot_cap), out_shap...  45.7 us

profile of v3, /device:TPU:0, one launch (start us, length us, event | category | flops | bytes accessed | tf_op | source)
XLA Modules:
  0.0 46.5 jit_solution(17024521430328650390)
XLA Ops:
  0.0 45.7 %shard_map.109 = bf16[2,128,1024]{2,1,0:T(8,128)(2,1)S(1)} custom-call(s32[1,2]{1,0:T(1,128)} %bitcast.19, s32[2,128]{1,0:T(2,128)} %bitcast.17, s32[2,128]{1,0:T(2,128)} %bitcast.18, bf16[32,1024]{1,0:T(8,128)(2,1)} %bitcast.15, bf16[1,1024]{1,0:T(2,128)(2,1)} %gain_hbm.1, bf16[32,1024]{1,0:T(8,128)(2,1)} %bitcast.16, bf16[2,128,1024]{2,1,0:T(8,128)(2,1)} %bitcast.13, ...), custom_call_target="tpu_custom_call" | custom-call | flops 1241513984 | bytes 8388608 | tf_op jit(solution)/shard_map/pallas_call | solution.py:358
  45.7 0.8 %copy.13 = bf16[1,2,128,1024]{3,2,1,0:T(8,128)(2,1)} copy(bf16[1,2,128,1024]{3,2,1,0:T(8,128)(2,1)S(1)} %bitcast.10) | data formatting | bytes 1048576
